TPU v7x, 32 devices: a whole 2x2x4 slice. The times are simulated.
32 devices in a mesh: dp: 4 (over z), row: 2 (over x), col: 4 (over y, core).
Axes of the slice: x: 2, y: 2, z: 4, core: 2. Of those that a mesh axis runs over, the one named last changes fastest.
Arguments:
- tokens: bfloat16 [2048, 1024], P(('dp', 'col'), 'row'), may hold values from -6 to 6
- seq_lengths: int32 [4, 3], P('dp'), may hold values from 1 to 448, 512 in all within a row
- norm1_gain: float32 [1024], P('row'), may hold values from 0.1 to 1.9
- w_query: bfloat16 [1024, 1024], P('row', 'col'), may hold values from -0.1875 to 0.1875
- w_key: bfloat16 [1024, 1024], P('row', 'col'), may hold values from -0.1875 to 0.1875
- w_value: bfloat16 [1024, 1024], P('row', 'col'), may hold values from -0.1875 to 0.1875
- b_query: float32 [1024], P('col'), may hold values from -3 to 3
- b_key: float32 [1024], P('col'), may hold values from -3 to 3
- b_value: float32 [1024], P('col'), may hold values from -3 to 3
- w_out: bfloat16 [1024, 1024], P('col', 'row'), may hold values from -1.5 to 1.5
- norm2_gain: float32 [1024], P('row'), may hold values from 0.1 to 1.9
- w_gate: bfloat16 [1024, 2816], P('row', 'col'), may hold values from -0.1875 to 0.1875
- w_up: bfloat16 [1024, 2816], P('row', 'col'), may hold values from -0.1875 to 0.1875
- w_down: bfloat16 [2816, 1024], P('col', 'row'), may hold values from -0.109375 to 0.109375
- cotangent: bfloat16 [2048, 1024], P(('dp', 'col'), 'row'), may hold values from -6 to 6
Outputs:
- layer_out: bfloat16 [2048, 1024], P(('dp', 'col'), 'row')
- d_tokens: bfloat16 [2048, 1024], P(('dp', 'col'), 'row')
- d_norm1_gain: float32 [1024], P('row')
- d_w_query: float32 [1024, 1024], P('row', 'col')
- d_w_key: float32 [1024, 1024], P('row', 'col')
- d_w_value: float32 [1024, 1024], P('row', 'col')
- d_b_query: float32 [1024], P('col')
- d_b_key: float32 [1024], P('col')
- d_b_value: float32 [1024], P('col')
- d_w_out: float32 [1024, 1024], P('col', 'row')
- d_norm2_gain: float32 [1024], P('row')
- d_w_gate: float32 [1024, 2816], P('row', 'col')
- d_w_up: float32 [1024, 2816], P('row', 'col')
- d_w_down: float32 [2816, 1024], P('col', 'row')
Inputs may be any that keep to these rules, and one draw needn't show every extreme that they name: `seq_lengths`: each row holds 3 lengths that sum to 512, one of them exactly 448.
All inputs are finite; a program needn't handle non-finite values.
Results may differ from a plain program's by a relative error of at most 0.035.
Values may be sent and summed in bfloat16 or wider, within the bound.
A program may use at most 128 MiB of HBM per device.

v0:
```python
import functools

import jax
import jax.numpy as jnp
from jax import lax
from jax.experimental import pallas as pl
from jax.experimental.pallas import tpu as pltpu
from jax.sharding import PartitionSpec as P

HEAD_DIM = 64
NORM_EPS = 1e-06
ROPE_THETA = 1000000.0
MESH = pl.DeviceIdType.MESH
F32 = jnp.float32
BF16 = jnp.bfloat16


def dot_plain(left, right):
    return jnp.dot(left, right, preferred_element_type=F32)


def dot_left_t(left, right):
    return lax.dot_general(left, right, (((0,), (0,)), ((), ())), preferred_element_type=F32)


def dot_right_t(left, right):
    return lax.dot_general(left, right, (((1,), (1,)), ((), ())), preferred_element_type=F32)


class Plane:
    def __init__(self, rows, cols):
        self.row = lax.axis_index("row")
        col = lax.axis_index("col")
        self.chip, self.core = col // 2, col % 2
        self.n_row, self.n_chip = rows, cols // 2
        self.offsets = [
            (dr, dc) for dr in range(rows) for dc in range(cols // 2) if (dr, dc) != (0, 0)
        ]

    def sibling(self):
        return {"row": self.row, "col": self.chip * 2 + 1 - self.core}

    def place(self, dr, dc, sign=1):
        return (
            lax.rem(self.row + sign * dr + self.n_row, self.n_row),
            lax.rem(self.chip + sign * dc + self.n_chip, self.n_chip),
        )

    def device(self, place):
        return {"row": place[0], "col": place[1] * 2 + self.core}

    def barrier(self, extra=()):
        sem = pltpu.get_barrier_semaphore()
        peers = [self.sibling()] + [self.device(self.place(*off)) for off in self.offsets]
        peers += list(extra)
        for peer in peers:
            pl.semaphore_signal(sem, inc=1, device_id=peer, device_id_type=MESH)
        pl.semaphore_wait(sem, len(peers))


def block_of(ref, place, core, height, width):
    top = pl.multiple_of((place[1] * 2 + core) * height, height)
    left = pl.multiple_of(place[0] * width, width)
    return ref.at[pl.ds(top, height), pl.ds(left, width)]


def remote(src, dst, send, recv, device):
    return pltpu.make_async_remote_copy(
        src_ref=src, dst_ref=dst, send_sem=send, recv_sem=recv, device_id=device, device_id_type=MESH
    )


def gather_start(plane, out, height, width, sems):
    sib_send, sib_recv, chip_send, chip_recv = sems
    here = (plane.row, plane.chip)
    own = block_of(out, here, plane.core, height, width)
    copies = []
    for k, off in enumerate(plane.offsets):
        copy = remote(own, own, chip_send.at[k], chip_recv.at[k], plane.device(plane.place(*off)))
        copy.start()
        copies.append(copy)
    last = len(plane.offsets)
    copy = remote(own, own, sib_send.at[last], sib_recv.at[last], plane.sibling())
    copy.start()
    copies.append(copy)
    return copies


def gather_end(plane, out, height, width, sems, copies):
    sib_send, sib_recv, chip_send, chip_recv = sems
    for k, off in enumerate(plane.offsets):
        block = block_of(out, plane.place(*off, sign=-1), plane.core, height, width)
        yield
        remote(block, block, chip_send.at[k], chip_recv.at[k], plane.sibling()).wait_recv()
        copy = remote(block, block, sib_send.at[k], sib_recv.at[k], plane.sibling())
        copy.start()
        copies.append(copy)
    for k, off in enumerate(plane.offsets + [(0, 0)]):
        block = block_of(out, plane.place(*off, sign=-1), 1 - plane.core, height, width)
        yield
        remote(block, block, sib_send.at[k], sib_recv.at[k], plane.sibling()).wait_recv()
    for copy in copies:
        copy.wait_send()


def run_all(*steps):
    steps = list(steps)
    while steps:
        for step in list(steps):
            try:
                next(step)
            except StopIteration:
                steps.remove(step)


def gather_kernel(rows, cols, count, *refs):
    ins, outs, sems = refs[:count], refs[count : 2 * count], refs[2 * count :]
    plane = Plane(rows, cols)
    height, width = ins[0].shape
    here = (plane.row, plane.chip)
    for src, out in zip(ins, outs):
        block_of(out, here, plane.core, height, width)[...] = src[...]
    plane.barrier()
    pending = []
    for i, out in enumerate(outs):
        own_sems = [sem.at[i] for sem in sems]
        pending.append((out, own_sems, gather_start(plane, out, height, width, own_sems)))
    run_all(*[gather_end(plane, out, height, width, own, copies) for out, own, copies in pending])


def reduce_steps(plane, part, addend, out, scratch):
    sib_buf, send_buf, recv_buf, s_send, s_recv, c_send, c_recv = scratch[:7]
    sems = scratch[7:]
    height, width = send_buf.shape[1:]
    here = (plane.row, plane.chip)
    sib_copies = []
    for dc in reversed(range(plane.n_chip)):
        chip = plane.place(0, dc)[1]
        top = pl.multiple_of((chip * 2 + 1 - plane.core) * height, height)
        copy = remote(
            part.at[pl.ds(top, height), :],
            sib_buf.at[dc],
            s_send.at[dc],
            s_recv.at[dc],
            plane.sibling(),
        )
        copy.start()
        sib_copies.append(copy)

    def both(place, dc):
        left = pl.multiple_of(place[0] * width, width)
        own = block_of(part, place, plane.core, height, width)[...]
        return own.astype(F32) + sib_buf[dc, :, pl.ds(left, width)].astype(F32)

    copies = []
    waited = set()
    order = sorted(range(len(plane.offsets)), key=lambda k: (-plane.offsets[k][1], -plane.offsets[k][0]))
    for k in order:
        dr, dc = plane.offsets[k]
        if dc not in waited:
            waited.add(dc)
            yield
            sib_copies[plane.n_chip - 1 - dc].wait_recv()
        place = plane.place(dr, dc)
        send_buf[k] = both(place, dc).astype(BF16)
        copy = remote(
            send_buf.at[k], recv_buf.at[k], c_send.at[k], c_recv.at[k], plane.device(place)
        )
        copy.start()
        copies.append(copy)
    if 0 not in waited:
        sib_copies[plane.n_chip - 1].wait_recv()
    total = both(here, 0)
    if addend is not None:
        total = total + addend[...].astype(F32)
    for copy in copies:
        yield
        copy.wait_recv()
    for k in range(len(plane.offsets)):
        total = total + recv_buf[k].astype(F32)
    if sems:
        block_of(out, here, plane.core, height, width)[...] = total.astype(out.dtype)
        pending = gather_start(plane, out, height, width, sems)
        yield from gather_end(plane, out, height, width, sems, pending)
    else:
        out[...] = total.astype(out.dtype)
    for copy in copies + sib_copies:
        copy.wait_send()


def reduce_kernel(rows, cols, part, addend, out, *scratch):
    plane = Plane(rows, cols)
    plane.barrier()
    run_all(reduce_steps(plane, part, addend, out, scratch))


class Ring:
    def __init__(self, count):
        self.count = count
        self.place = lax.axis_index("dp")
        self.next = {"dp": self.at(1)}

    def at(self, offset):
        return lax.rem(self.place + offset + 2 * self.count, self.count)


def ring_sum_steps(ring, pieces, out, recv, send_sem, recv_sem):
    copies = []
    for step in range(ring.count - 1):
        if step == 0:
            src = pieces.at[:, ring.at(-1)]
        else:
            src = recv.at[step - 1]
        copy = remote(src, recv.at[step], send_sem.at[step], recv_sem.at[step], ring.next)
        copy.start()
        copies.append(copy)
        yield
        copy.wait_recv()
        total = recv[step].astype(F32) + pieces[:, ring.at(-step - 2)].astype(F32)
        if step < ring.count - 2:
            recv[step] = total.astype(BF16)
        else:
            out[...] = total.astype(BF16)
    for copy in copies:
        copy.wait_send()


def ring_gather_steps(ring, plane, chunk, out, row_sems, send_sem, recv_sem):
    swap = remote(
        chunk.at[1 - plane.row],
        out.at[ring.place, plane.row],
        row_sems.at[0],
        row_sems.at[1],
        plane.device((1 - plane.row, plane.chip)),
    )
    swap.start()
    out[ring.place, plane.row] = chunk[plane.row]
    yield
    landed = out.at[ring.place, 1 - plane.row]
    remote(landed, landed, row_sems.at[0], row_sems.at[1], ring.next).wait_recv()
    copies = [swap]
    for step in range(ring.count - 1):
        src = out.at[ring.at(-step)]
        copy = remote(src, src, send_sem.at[step], recv_sem.at[step], ring.next)
        copy.start()
        copies.append(copy)
        yield
        came = out.at[ring.at(-step - 1)]
        remote(came, came, send_sem.at[step], recv_sem.at[step], ring.next).wait_recv()
    for copy in copies:
        copy.wait_send()


def mlp_kernel(rows, cols, count, pieces_count, *refs):
    part, pieces = refs[0], refs[1 : 1 + pieces_count]
    refs = refs[1 + pieces_count :]
    out, chunks = refs[0], refs[1 : 1 + pieces_count]
    refs = refs[1 + pieces_count :]
    recvs, refs = refs[:pieces_count], refs[pieces_count:]
    ring_send, ring_recv = refs[:2]
    plane, ring = Plane(rows, cols), Ring(count)
    plane.barrier([ring.next, {"dp": ring.at(-1)}])
    run_all(
        reduce_steps(plane, part, None, out, refs[2:]),
        *[
            ring_sum_steps(ring, piece, chunk, recv, ring_send.at[i], ring_recv.at[i])
            for i, (piece, chunk, recv) in enumerate(zip(pieces, chunks, recvs))
        ],
    )


def last_kernel(rows, cols, count, n_mlp, n_att, *refs):
    refs = list(refs)

    def take(number):
        taken = refs[:number]
        del refs[:number]
        return taken

    part, part_out, h1_block, unit, small = take(5)
    mlp_chunks, pieces = take(n_mlp), take(n_att)
    d_normed, layer_out, small_out = take(3)
    mlp_outs, att_outs = take(n_mlp), take(n_att)
    recvs, chunks = take(n_att), take(n_att)
    small_buf, small_send, small_recv, small_row = take(4)
    row_sems, gather_send, gather_recv, ring_send, ring_recv = take(5)
    normed_scratch, out_scratch = take(11), take(7)
    plane, ring = Plane(rows, cols), Ring(count)
    others = [{"dp": ring.at(i)} for i in range(1, count)]
    plane.barrier(others)
    width = h1_block.shape[1]

    def attention(i):
        yield from ring_sum_steps(
            ring, pieces[i], chunks[i], recvs[i], ring_send.at[i], ring_recv.at[i]
        )
        k = n_mlp + i
        yield from ring_gather_steps(
            ring, plane, chunks[i], att_outs[i], row_sems.at[k], gather_send.at[k], gather_recv.at[k]
        )

    def normed():
        yield from reduce_steps(plane, part, None, d_normed, normed_scratch)
        left = pl.multiple_of(plane.row * width, width)
        gain = jnp.sum(d_normed[:, pl.ds(left, width)].astype(F32) * unit[...], axis=0, keepdims=True)
        first = lax.broadcasted_iota(jnp.int32, small.shape, 0) == 0
        small_buf[0] = jnp.where(first, gain, small[...])
        copies = []
        for i, other in enumerate(others):
            copy = remote(
                small_buf.at[0], small_buf.at[i + 1], small_send.at[i], small_recv.at[i], other
            )
            copy.start()
            copies.append(copy)
        for copy in copies:
            yield
            copy.wait()
        total = small_buf[0]
        for i in range(1, count):
            total = total + small_buf[i]
        small_out[plane.row] = total
        here = small_out.at[plane.row]
        pair = plane.device((1 - plane.row, plane.chip))
        copy = remote(here, here, small_row.at[0], small_row.at[1], pair)
        copy.start()
        yield
        there = small_out.at[1 - plane.row]
        remote(there, there, small_row.at[0], small_row.at[1], pair).wait_recv()
        copy.wait_send()

    gathers = [
        ring_gather_steps(
            ring, plane, mlp_chunks[i], mlp_outs[i], row_sems.at[i], gather_send.at[i], gather_recv.at[i]
        )
        for i in range(n_mlp)
    ]
    run_all(
        *[attention(i) for i in range(n_att)],
        *gathers,
        normed(),
        reduce_steps(plane, part_out, h1_block, layer_out, out_scratch),
    )


def dma(*shape):
    return pltpu.SemaphoreType.DMA(shape)


def params(collective_id):
    return pltpu.CompilerParams(
        collective_id=collective_id, has_side_effects=True, vmem_limit_bytes=32 << 20
    )


VMEM = pl.BlockSpec(memory_space=pltpu.VMEM)


def plane_gather(blocks, collective_id):
    rows, cols = lax.axis_size("row"), lax.axis_size("col")
    chips = rows * cols // 2
    count = len(blocks)
    height, width = blocks[0].shape
    return pl.pallas_call(
        functools.partial(gather_kernel, rows, cols, count),
        out_shape=[jax.ShapeDtypeStruct((height * cols, width * rows), b.dtype) for b in blocks],
        in_specs=[VMEM] * count,
        out_specs=[VMEM] * count,
        scratch_shapes=[dma(count, chips), dma(count, chips), dma(count, chips), dma(count, chips)],
        compiler_params=params(collective_id),
        name=f"plane_gather_{collective_id}",
    )(*blocks)


def reduce_scratch(rows, cols, height, width, gather):
    chips = rows * cols // 2
    scratch = [
        pltpu.VMEM((cols // 2, height, width * rows), BF16),
        pltpu.VMEM((chips - 1, height, width), BF16),
        pltpu.VMEM((chips - 1, height, width), BF16),
        dma(cols // 2),
        dma(cols // 2),
        dma(chips - 1),
        dma(chips - 1),
    ]
    if gather:
        scratch += [dma(chips), dma(chips), dma(chips), dma(chips)]
    return scratch


def call(kernel, ins, outs, scratch, collective_id, name):
    return pl.pallas_call(
        kernel,
        out_shape=outs,
        in_specs=[VMEM] * len(ins),
        out_specs=[VMEM] * len(outs),
        scratch_shapes=scratch,
        compiler_params=params(collective_id),
        name=name,
    )(*ins)


def shape(dims, dtype=BF16):
    return jax.ShapeDtypeStruct(tuple(dims), dtype)


def plane_reduce(part, addend):
    rows, cols = lax.axis_size("row"), lax.axis_size("col")
    height, width = addend.shape
    return call(
        functools.partial(reduce_kernel, rows, cols),
        [part, addend],
        [shape(part.shape)],
        reduce_scratch(rows, cols, height, width, True),
        1,
        "out_projection_reduce",
    )[0]


def mlp_back_reduce(part, pieces):
    rows, cols, count = lax.axis_size("row"), lax.axis_size("col"), lax.axis_size("dp")
    height, width = part.shape[0] // cols, part.shape[1] // rows
    chunks = [(p.shape[0],) + p.shape[2:] for p in pieces]
    scratch = [pltpu.VMEM((count - 1,) + c, BF16) for c in chunks]
    scratch += [dma(len(pieces), count - 1), dma(len(pieces), count - 1)]
    scratch += reduce_scratch(rows, cols, height, width, True)
    outs = call(
        functools.partial(mlp_kernel, rows, cols, count, len(pieces)),
        [part] + pieces,
        [shape(part.shape)] + [shape(c) for c in chunks],
        scratch,
        2,
        "mlp_back_reduce",
    )
    return outs[0], list(outs[1:])


def last_exchange(part, part_out, h1_block, unit, small, mlp_chunks, pieces):
    rows, cols, count = lax.axis_size("row"), lax.axis_size("col"), lax.axis_size("dp")
    height, width = h1_block.shape
    n_mlp, n_att = len(mlp_chunks), len(pieces)
    chunks = [(p.shape[0],) + p.shape[2:] for p in pieces]
    outs = [shape(part.shape), shape(h1_block.shape), shape((rows,) + small.shape, F32)]
    outs += [shape((count,) + c.shape) for c in mlp_chunks]
    outs += [shape((count,) + c) for c in chunks]
    scratch = [pltpu.VMEM((count - 1,) + c, BF16) for c in chunks]
    scratch += [pltpu.VMEM(c, BF16) for c in chunks]
    scratch += [pltpu.VMEM((count,) + small.shape, F32), dma(count - 1), dma(count - 1), dma(2)]
    scratch += [dma(n_mlp + n_att, 2), dma(n_mlp + n_att, count - 1), dma(n_mlp + n_att, count - 1)]
    scratch += [dma(n_att, count - 1), dma(n_att, count - 1)]
    scratch += reduce_scratch(rows, cols, height, width, True)
    scratch += reduce_scratch(rows, cols, height, width, False)
    outs = call(
        functools.partial(last_kernel, rows, cols, count, n_mlp, n_att),
        [part, part_out, h1_block, unit, small] + mlp_chunks + pieces,
        outs,
        scratch,
        3,
        "last_exchange",
    )
    return outs[0], outs[1], outs[2], outs[3:]


def swap_rows(value):
    return lax.ppermute(value, "row", [(0, 1), (1, 0)])


def half_of(value, index, axis):
    size = value.shape[axis] // 2
    return lax.dynamic_slice_in_dim(value, index * size, size, axis)


def in_order(row, own, other, axis):
    return jnp.where(
        row == 0,
        jnp.concatenate([own, other], axis),
        jnp.concatenate([other, own], axis),
    )


def whole_of_half(weight, row, cut, join):
    other = swap_rows(half_of(weight, 1 - row, cut))
    return in_order(row, half_of(weight, row, cut), other, join)


def unit_of(values):
    inverse = lax.rsqrt(jnp.mean(values * values, axis=1, keepdims=True) + NORM_EPS)
    return values * inverse, inverse


def norm_back(d_normed, gain, unit, inverse):
    scaled = d_normed * gain
    inner = jnp.sum(scaled * unit, axis=1, keepdims=True)
    return inverse * (scaled - unit * (inner / unit.shape[1]))


def layout(lengths, group_len):
    seq_ends = jnp.cumsum(lengths)
    token_place = jnp.arange(group_len, dtype=jnp.int32)
    seq_ids = jnp.sum((token_place[:, None] >= seq_ends[None, :]).astype(jnp.int32), axis=1)
    seq_starts = seq_ends - lengths
    onehot = (seq_ids[:, None] == jnp.arange(lengths.shape[0], dtype=jnp.int32)[None, :]).astype(
        jnp.int32
    )
    position = token_place - jnp.sum(onehot * seq_starts[None, :], axis=1)
    allowed = (seq_ids[:, None] == seq_ids[None, :]) & (
        token_place[None, :] <= token_place[:, None]
    )
    freqs = ROPE_THETA ** (-(jnp.arange(HEAD_DIM // 2, dtype=F32) * 2.0 / HEAD_DIM))
    angles = position.astype(F32)[:, None] * freqs[None, :]
    return (jnp.cos(angles), jnp.sin(angles), allowed)


def rotate(values, rot_cos, rot_sin):
    half_dim = HEAD_DIM // 2
    first, second = values[..., :half_dim], values[..., half_dim:]
    return jnp.concatenate(
        [first * rot_cos - second * rot_sin, second * rot_cos + first * rot_sin], axis=-1
    )


def to_heads(values):
    return [values[:, i : i + HEAD_DIM] for i in range(0, values.shape[1], HEAD_DIM)]


def in_chunks(grad):
    count = lax.axis_size("dp")
    grad = grad.astype(BF16)
    return grad.reshape(2, count, grad.shape[0] // (2 * count), grad.shape[1])


def from_chunks(summed):
    return summed.transpose(0, 2, 1, 3).reshape(-1, 2 * summed.shape[3]).astype(F32)


def on_device(
    tokens,
    seq_lengths,
    norm1_gain,
    w_query,
    w_key,
    w_value,
    b_query,
    b_key,
    b_value,
    w_out,
    norm2_gain,
    w_gate,
    w_up,
    w_down,
    cotangent,
):
    height, width = tokens.shape
    row, col = lax.axis_index("row"), lax.axis_index("col")
    rows, cols = lax.axis_size("row"), lax.axis_size("col")
    group_len = height * cols
    scale = HEAD_DIM ** (-0.5)

    def own_block(full):
        return lax.dynamic_slice(full, (col * height, row * width), (height, width))

    def joined_half(parts):
        return jnp.concatenate([half_of(part, row, 0) for part in parts])

    w_qkv_own = jnp.concatenate([half_of(w, row, 1) for w in (w_query, w_key, w_value)], 1)
    w_qkv_other = swap_rows(
        jnp.concatenate([half_of(w, 1 - row, 1) for w in (w_query, w_key, w_value)], 1)
    )
    w_qkv = in_order(row, w_qkv_own, w_qkv_other, 0)
    gains = jnp.stack([norm1_gain, norm2_gain])
    gains = in_order(row, gains, swap_rows(gains), 1)
    w_o = whole_of_half(w_out, row, 0, 1)
    w_g = whole_of_half(w_gate, row, 1, 0)
    w_u = whole_of_half(w_up, row, 1, 0)
    w_d = whole_of_half(w_down, row, 0, 1)

    token_full, cot_full = plane_gather([tokens, cotangent], 0)
    resid = token_full.astype(F32)
    unit_one, inverse_one = unit_of(resid)
    normed_one = (unit_one * gains[0:1]).astype(BF16)
    qkv = dot_plain(normed_one, w_qkv) + joined_half((b_query, b_key, b_value))
    own_cols = qkv.shape[1] // 3
    rot_cos, rot_sin, allowed = layout(seq_lengths[0], group_len)
    q_heads = [rotate(h, rot_cos, rot_sin).astype(BF16) for h in to_heads(qkv[:, :own_cols])]
    k_heads = [
        rotate(h, rot_cos, rot_sin).astype(BF16) for h in to_heads(qkv[:, own_cols : 2 * own_cols])
    ]
    v_heads = [h.astype(BF16) for h in to_heads(qkv[:, 2 * own_cols :])]
    head_outs, head_probs = [], []
    for query, keys, values in zip(q_heads, k_heads, v_heads):
        scores = jnp.where(allowed, dot_right_t(query, keys) * scale, -1000000000.0)
        expo = jnp.exp(scores - jnp.max(scores, axis=-1, keepdims=True))
        probs = expo / jnp.sum(expo, axis=-1, keepdims=True)
        head_probs.append(probs)
        head_outs.append(dot_plain(probs.astype(BF16), values).astype(BF16))
    heads = jnp.concatenate(head_outs, 1)
    h1_full = plane_reduce(dot_plain(heads, w_o).astype(BF16), tokens)
    unit_two, inverse_two = unit_of(h1_full.astype(F32))
    normed_two = (unit_two * gains[1:2]).astype(BF16)
    gate, upper = dot_plain(normed_two, w_g), dot_plain(normed_two, w_u)
    sigmoid_gate = jax.nn.sigmoid(gate)
    silu_gate = gate * sigmoid_gate
    hidden = (silu_gate * upper).astype(BF16)
    d_hidden = dot_right_t(cot_full, w_d).astype(BF16).astype(F32)
    d_gate = (d_hidden * upper * sigmoid_gate * (1.0 + gate * (1.0 - sigmoid_gate))).astype(BF16)
    d_upper = (d_hidden * silu_gate).astype(BF16)
    part = (dot_right_t(d_gate, w_g) + dot_right_t(d_upper, w_u)).astype(BF16)
    pieces = [dot_left_t(normed_two, d_gate), dot_left_t(normed_two, d_upper)]
    pieces.append(dot_left_t(cot_full, hidden))
    d_normed_two, mlp_chunks = mlp_back_reduce(part, [in_chunks(p) for p in pieces])
    d_normed_two = d_normed_two.astype(F32)
    d_h1 = norm_back(d_normed_two, gains[1:2], unit_two, inverse_two) + cot_full.astype(F32)
    own_half = row * width
    d_gain_two = jnp.sum(d_normed_two * unit_two, axis=0)
    d_gain_two = lax.dynamic_slice_in_dim(d_gain_two, own_half, width)

    d_branch = d_h1.astype(BF16)
    d_heads = dot_right_t(d_branch, w_o).astype(BF16)
    d_q, d_k, d_v = [], [], []
    for query, keys, values, probs, d_out in zip(
        q_heads, k_heads, v_heads, head_probs, to_heads(d_heads)
    ):
        d_v.append(dot_left_t(probs.astype(BF16), d_out))
        d_probs = dot_right_t(d_out, values)
        d_scores = (
            probs * (d_probs - jnp.sum(probs * d_probs, axis=-1, keepdims=True))
        ).astype(BF16)
        d_q.append(rotate(dot_plain(d_scores, keys) * scale, rot_cos, -rot_sin))
        d_k.append(rotate(dot_left_t(d_scores, query) * scale, rot_cos, -rot_sin))
    d_qkv = jnp.concatenate(d_q + d_k + d_v, 1).astype(BF16)
    part = dot_right_t(d_qkv, w_qkv).astype(BF16)
    pieces = [
        in_chunks(dot_left_t(normed_one, d_qkv[:, i * own_cols : (i + 1) * own_cols]))
        for i in range(3)
    ]
    pieces.append(in_chunks(dot_left_t(d_branch, heads)))
    d_bias = jnp.sum(d_qkv.astype(F32), axis=0)
    small = jnp.zeros((8, width), F32)
    small = small.at[1].set(d_gain_two)
    small = small.at[2:5, :own_cols].set(d_bias.reshape(3, own_cols))
    unit_own = lax.dynamic_slice_in_dim(unit_one, own_half, width, 1)
    part_out = dot_plain(hidden, w_d).astype(BF16)
    d_normed_one, layer_out, small, summed = last_exchange(
        part, part_out, own_block(h1_full), unit_own, small, mlp_chunks, pieces
    )
    d_tokens = norm_back(d_normed_one.astype(F32), gains[0:1], unit_one, inverse_one) + d_h1
    d_tokens = own_block(d_tokens.astype(BF16))
    own_small = lax.dynamic_index_in_dim(small, row, 0, keepdims=False)
    bias_sum = [small[:, 2 + i, :own_cols].reshape(-1) for i in range(3)]
    summed = [from_chunks(item) for item in summed]
    return (
        layer_out,
        d_tokens,
        own_small[0],
        summed[3],
        summed[4],
        summed[5],
        bias_sum[0],
        bias_sum[1],
        bias_sum[2],
        summed[6].T,
        own_small[1],
        summed[0],
        summed[1],
        summed[2].T,
    )


def solution(mesh):
    block = P(("dp", "col"), "row")
    down, across = P("row", "col"), P("col", "row")
    return jax.shard_map(
        on_device,
        mesh=mesh,
        in_specs=(
            block,
            P("dp", None),
            P("row"),
            down,
            down,
            down,
            P("col"),
            P("col"),
            P("col"),
            across,
            P("row"),
            down,
            down,
            across,
            block,
        ),
        out_specs=(
            block,
            block,
            P("row"),
            down,
            down,
            down,
            P("col"),
            P("col"),
            P("col"),
            across,
            P("row"),
            down,
            down,
            across,
        ),
        check_vma=False,
    )
```

profile of v0, /device:TPU:0, one launch (start us, length us, event | category | flops | bytes accessed | tf_op | source)
XLA Modules:
  0.0 289.2 jit_solution(10543816766050488861)
XLA Ops:
  2.5 1.8 constant_dynamic-slice_fusion.14
  5.1 2.9 %collective-permute-start.1 = (bf16[512,384]{1,0:T(8,128)(2,1)}, bf16[512,384]{1,0:T(8,128)(2,1)}, u32[]{:S(2)}, u32[]{:S(2)}) collective-permute-start(bf16[512,384]{1,0:T(8,128)(2,1)} %pad_maximum_fusion), channel_id=1, source_target_pairs={{0,4},{4,0},{1,5},{5,1},{2,6},{6,2},{3,7},{7,3},{8,12},{12,8},{9,1... | collective-permute-start | bytes 1179656 | tf_op jit(solution)/shard_map/ppermute | solution.py:464
  9.1 2.0 collective-permute-start.5
  12.7 2.0 collective-permute-start.3
  14.9 34.5 %plane_gather_0.1 = (bf16[512,1024]{1,0:T(8,128)(2,1)S(1)}, bf16[512,1024]{1,0:T(8,128)(2,1)S(1)}) custom-call(bf16[128,512]{1,0:T(8,128)(2,1)S(1)} %copy-done.9, bf16[128,512]{1,0:T(8,128)(2,1)S(1)} %copy-done.14), custom_call_target="tpu_custom_call" | custom-call | tf_op jit(solution)/shard_map/plane_gather_0/pallas_call | solution.py:363
  56.2 1.9 fusion.13
  58.2 1.9 fusion.160
  65.9 19.5 %out_projection_reduce.1 = bf16[512,1024]{1,0:T(8,128)(2,1)S(1)} custom-call(bf16[512,1024]{1,0:T(8,128)(2,1)S(1)} %convolution_convert_fusion.part, bf16[128,512]{1,0:T(8,128)(2,1)S(1)} %copy-done.9), custom_call_target="tpu_custom_call" | custom-call | tf_op jit(solution)/shard_map/out_projection_reduce/pallas_call | solution.py:391
  85.7 1.8 fusion.45
  91.7 2.3 copy.43
  94.0 2.5 convolution_convert_fusion.4
  96.5 2.3 copy.44
  98.8 2.8 convolution_convert_fusion.3
  101.5 2.3 copy.45
  103.8 2.2 fusion.46
  106.1 2.0 add_convert_fusion.refs_0_
  108.1 53.0 %mlp_back_reduce.1 = (bf16[512,1024]{1,0:T(8,128)(2,1)S(1)}, bf16[2,128,352]{2,1,0:T(8,128)(2,1)S(1)}, bf16[2,128,352]{2,1,0:T(8,128)(2,1)S(1)}, bf16[2,128,352]{2,1,0:T(8,128)(2,1)S(1)}) custom-call(bf16[512,1024]{1,0:T(8,128)(2,1)S(1)} %add_convert_fusion.refs_0_, bf16[2,4,128,352]{3,2,1,0:T(8,128)(2,1)S(1)} %bitcast.100, ...), custom_call_target="tpu_custom_call" | custom-call | tf_op jit(solution)/shard_map/mlp_back_reduce/pallas_call | solution.py:391
  162.9 1.9 convolution_convert_fusion.11
  176.3 1.9 convolution_convert_fusion.2.refs_0_
  178.3 1.9 convolution_convert_fusion.1.refs_1_
  180.3 84.6 %last_exchange.1 = (bf16[512,1024]{1,0:T(8,128)(2,1)S(1)}, bf16[128,512]{1,0:T(8,128)(2,1)S(1)}, f32[2,8,512]{2,1,0:T(8,128)S(1)}, bf16[4,2,128,352]{3,2,1,0:T(8...) custom-call(bf16[512,1024]{1,0:T(8,128)(2,1)S(1)} %convolution_conve, ...), custom_call_target="tpu_custom_call" | custom-call | tf_op jit(solution)/shard_map/last_exchange/pallas_call | solution.py:391
  264.9 1.9 multiply_reduce_fusion
  283.4 2.6 copy.68
  286.6 1.9 fusion.22
  (257 shorter events, 52.9 us)
Async XLA Ops:
  0.6 7.4 %copy-start.59 = (f32[512]{0:T(512)S(1)}, f32[512]{0:T(512)}, u32[]{:S(2)}) copy-start(f32[512]{0:T(512)} %param.29) | copy-start | bytes 6148
  0.7 7.4 %copy-start.60 = (f32[512]{0:T(512)S(1)}, f32[512]{0:T(512)}, u32[]{:S(2)}) copy-start(f32[512]{0:T(512)} %param.21) | copy-start | bytes 6148
  0.7 7.5 %copy-start.22 = (bf16[512,704]{0,1:T(8,128)(2,1)S(1)}, bf16[512,704]{0,1:T(8,128)(2,1)}, u32[]{:S(2)}) copy-start(bf16[512,704]{0,1:T(8,128)(2,1)} %param.30) | copy-start | bytes 2162692
  0.7 10.4 %copy-start.32 = (bf16[256,512]{1,0:T(8,128)(2,1)S(1)}, bf16[256,512]{1,0:T(8,128)(2,1)}, u32[]{:S(2)}) copy-start(bf16[256,512]{1,0:T(8,128)(2,1)} %param.28) | copy-start | bytes 786436
  0.7 11.1 %copy-start.23 = (bf16[704,512]{1,0:T(8,128)(2,1)S(1)}, bf16[704,512]{1,0:T(8,128)(2,1)}, u32[]{:S(2)}) copy-start(bf16[704,512]{1,0:T(8,128)(2,1)} %param.32) | copy-start | bytes 2162692
  4.3 10.4 %copy-start.71 = (f32[256]{0:T(256)S(1)}, f32[256]{0:T(256)}, u32[]{:S(2)}) copy-start(f32[256]{0:T(256)} %param.27) | copy-start | bytes 3076
  4.3 10.5 %copy-start.72 = (f32[256]{0:T(256)S(1)}, f32[256]{0:T(256)}, u32[]{:S(2)}) copy-start(f32[256]{0:T(256)} %param.26) | copy-start | bytes 3076
  4.3 10.5 %copy-start.73 = (f32[256]{0:T(256)S(1)}, f32[256]{0:T(256)}, u32[]{:S(2)}) copy-start(f32[256]{0:T(256)} %param.25) | copy-start | bytes 3076
  4.3 10.6 %copy-start.9 = (bf16[128,512]{1,0:T(8,128)(2,1)S(1)}, bf16[128,512]{1,0:T(8,128)(2,1)}, u32[]{:S(2)}) copy-start(bf16[128,512]{1,0:T(8,128)(2,1)} %addend.1) | copy-start | bytes 393220
  4.3 10.6 %copy-start.14 = (bf16[128,512]{1,0:T(8,128)(2,1)S(1)}, bf16[128,512]{1,0:T(8,128)(2,1)}, u32[]{:S(2)}) copy-start(bf16[128,512]{1,0:T(8,128)(2,1)} %refs_1_.1) | copy-start | bytes 393220
  5.1 53.0 %collective-permute-start.1 = (bf16[512,384]{1,0:T(8,128)(2,1)}, bf16[512,384]{1,0:T(8,128)(2,1)}, u32[]{:S(2)}, u32[]{:S(2)}) collective-permute-start(bf16[512,384]{1,0:T(8,128)(2,1)} %pad_maximum_fusion), channel_id=1, source_target_pairs={{0,4},{4,0},{1,5},{5,1},{2,6},{6,2},{3,7},{7,3},{8,12},{12,8},{9,1... | collective-permute-start | bytes 1179656 | tf_op jit(solution)/shard_map/ppermute | solution.py:464
  8.1 46.5 %collective-permute-start = (f32[2,512]{1,0:T(2,128)S(1)}, f32[2,512]{1,0:T(2,128)S(1)}, u32[]{:S(2)}, u32[]{:S(2)}) collective-permute-start(f32[2,512]{1,0:T(2,128)S(1)} %pad_maximum_fusion.16), channel_id=1, source_target_pairs={{0,4},{4,0},{1,5},{5,1},{2,6},{6,2},{3,7},{7,3},{8,12},{12,8},{9,1... | collective-permute-start | bytes 12296 | tf_op jit(solution)/shard_map/ppermute | solution.py:464
  8.2 41.6 %copy-start.74 = (s32[1,3]{1,0:T(1,128)S(1)}, s32[1,3]{1,0:T(1,128)}, u32[]{:S(2)}) copy-start(s32[1,3]{1,0:T(1,128)} %param.20) | copy-start | bytes 40
  9.1 41.0 %copy-start.24 = (bf16[512,704]{0,1:T(8,128)(2,1)S(1)}, bf16[512,704]{0,1:T(8,128)(2,1)}, u32[]{:S(2)}) copy-start(bf16[512,704]{0,1:T(8,128)(2,1)} %param.31) | copy-start | bytes 2162692
  9.1 76.6 %collective-permute-start.5 = (bf16[512,352]{0,1:T(8,128)(2,1)}, bf16[512,352]{0,1:T(8,128)(2,1)}, u32[]{:S(2)}, u32[]{:S(2)}) collective-permute-start(bf16[512,352]{0,1:T(8,128)(2,1)} %get-tuple-element.132), channel_id=1, source_target_pairs={{0,4},{4,0},{1,5},{5,1},{2,6},{6,2},{3,7},{7,3},{8,12},{12,8},{9,1... | collective-permute-start | bytes 1081352 | tf_op jit(solution)/shard_map/ppermute | solution.py:464
  11.8 52.1 %copy-start.25 = (bf16[128,512]{1,0:T(8,128)(2,1)}, bf16[128,512]{1,0:T(8,128)(2,1)S(1)}, u32[]{:S(2)}) copy-start(bf16[128,512]{1,0:T(8,128)(2,1)S(1)} %get-tuple-element.135) | copy-start | bytes 393220
  11.8 52.1 %collective-permute-start.2 = (bf16[128,512]{1,0:T(8,128)(2,1)}, bf16[128,512]{1,0:T(8,128)(2,1)}, u32[]{:S(2)}, u32[]{:S(2)}) collective-permute-start(bf16[128,512]{1,0:T(8,128)(2,1)} %get-tuple-element.136), channel_id=1, source_target_pairs={{0,4},{4,0},{1,5},{5,1},{2,6},{6,2},{3,7},{7,3},{8,12},{12,8},{9,1... | collective-permute-start | bytes 393224 | tf_op jit(solution)/shard_map/ppermute | solution.py:464
  12.7 43.4 %collective-permute-start.3 = (bf16[352,512]{1,0:T(8,128)(2,1)}, bf16[352,512]{1,0:T(8,128)(2,1)}, u32[]{:S(2)}, u32[]{:S(2)}) collective-permute-start(bf16[352,512]{1,0:T(8,128)(2,1)} %get-tuple-element.134), channel_id=1, source_target_pairs={{0,4},{4,0},{1,5},{5,1},{2,6},{6,2},{3,7},{7,3},{8,12},{12,8},{9,1... | collective-permute-start | bytes 1081352 | tf_op jit(solution)/shard_map/ppermute | solution.py:464
  49.5 6.7 %copy-start = (bf16[512,1024]{1,0:T(8,128)(2,1)}, bf16[512,1024]{1,0:T(8,128)(2,1)S(1)}, u32[]{:S(2)}) copy-start(bf16[512,1024]{1,0:T(8,128)(2,1)S(1)} %get-tuple-element.55) | copy-start | bytes 3145732
  49.8 8.4 %copy-start.55 = (f32[512]{0:T(512)}, f32[512]{0:T(512)S(1)}, u32[]{:S(2)}) copy-start(f32[512]{0:T(512)S(1)} %add_rsqrt_fusion.1) | copy-start | bytes 6148
  54.6 33.0 %collective-permute-start.4 = (bf16[512,352]{0,1:T(8,128)(2,1)}, bf16[512,352]{0,1:T(8,128)(2,1)S(1)}, u32[]{:S(2)}, u32[]{:S(2)}) collective-permute-start(bf16[512,352]{0,1:T(8,128)(2,1)} %get-tuple-element.130), channel_id=1, source_target_pairs={{0,4},{4,0},{1,5},{5,1},{2,6},{6,2},{3,7},{7,3},{8,12},{12,8},{9,1... | collective-permute-start | bytes 1081352 | tf_op jit(solution)/shard_map/ppermute | solution.py:464
  64.5 21.3 %copy-start.28 = (bf16[512,352]{0,1:T(8,128)(2,1)S(1)}, bf16[512,352]{0,1:T(8,128)(2,1)}, u32[]{:S(2)}) copy-start(bf16[512,352]{0,1:T(8,128)(2,1)} %get-tuple-element.131) | copy-start | bytes 1081348
  108.1 53.8 %copy-start.1 = (bf16[512,1024]{1,0:T(8,128)(2,1)S(1)}, bf16[512,1024]{1,0:T(8,128)(2,1)}, u32[]{:S(2)}) copy-start(bf16[512,1024]{1,0:T(8,128)(2,1)} %copy-done) | copy-start | bytes 3145732
  162.9 6.8 %copy-start.17 = (f32[512,1024]{1,0:T(8,128)}, f32[512,1024]{1,0:T(8,128)S(1)}, u32[]{:S(2)}) copy-start(f32[512,1024]{1,0:T(8,128)S(1)} %fusion.5) | copy-start | bytes 6291460
  (60 other events, 95.8 us)
where the time goes:
time: 290 us; the launch traced here: 289 us
  Pallas kernels  192 us (66%)
  local copies, waits for them, and re-layouts  38 us (13%)
  matrix products  33.7 us (12%)
  other arithmetic  15.5 us (5%)
  starting transfers between devices  8.53 us (3%)
    pallas_call x3, Pallas kernels, call(): pl.pallas_call(kernel, out_shape=outs, in_specs=[VMEM] * len(ins), out_sp...  157 us
    pallas_call x1, Pallas kernels, plane_gather(): pl.pallas_call(functools.partial(gather_kernel, rows, cols, count), out_s...  34.5 us
    dot_general x9, matrix products, dot_right_t(): lax.dot_general(left, right, (((1,), (1,)), ((), ())), preferred_element_...  13.3 us
    unnamed x165, local copies, waits for them, and re-layouts  13.3 us
    dot_general x11, matrix products, dot_left_t(): lax.dot_general(left, right, (((0,), (0,)), ((), ())), preferred_element_...  10.4 us
    dot_general x9, matrix products, dot_plain(): return jnp.dot(left, right, preferred_element_type=F32)  9.93 us
    ppermute x6, starting transfers between devices, swap_rows(): return lax.ppermute(value, 'row', [(0, 1), (1, 0)])  8.53 us
    dynamic_slice x9, local copies, waits for them, and re-layouts, half_of(): return lax.dynamic_slice_in_dim(value, index * size, size, axis)  7.22 us
  transfers between devices with their start and end apart: 6, of which 0 were waited for; matrix products, arithmetic and copies ran while one was open for 6% of the time, Pallas kernels for 19%

commit v1 on v0

--- a/solution.py
+++ b/solution.py
@@ -195,13 +195,13 @@
 
 
 class Ring:
-    def __init__(self, count):
-        self.count = count
+    def __init__(self, count, sign=1):
+        self.count, self.sign = count, sign
         self.place = lax.axis_index("dp")
         self.next = {"dp": self.at(1)}
 
     def at(self, offset):
-        return lax.rem(self.place + offset + 2 * self.count, self.count)
+        return lax.rem(self.place + self.sign * offset + 2 * self.count, self.count)
 
 
 def ring_sum_steps(ring, pieces, out, recv, send_sem, recv_sem):
@@ -259,11 +259,12 @@
     recvs, refs = refs[:pieces_count], refs[pieces_count:]
     ring_send, ring_recv = refs[:2]
     plane, ring = Plane(rows, cols), Ring(count)
+    rings = [ring, Ring(count, -1)]
     plane.barrier([ring.next, {"dp": ring.at(-1)}])
     run_all(
         reduce_steps(plane, part, None, out, refs[2:]),
         *[
-            ring_sum_steps(ring, piece, chunk, recv, ring_send.at[i], ring_recv.at[i])
+            ring_sum_steps(rings[i % 2], piece, chunk, recv, ring_send.at[i], ring_recv.at[i])
             for i, (piece, chunk, recv) in enumerate(zip(pieces, chunks, recvs))
         ],
     )
@@ -286,17 +287,18 @@
     row_sems, gather_send, gather_recv, ring_send, ring_recv = take(5)
     normed_scratch, out_scratch = take(11), take(7)
     plane, ring = Plane(rows, cols), Ring(count)
+    rings = [ring, Ring(count, -1)]
     others = [{"dp": ring.at(i)} for i in range(1, count)]
     plane.barrier(others)
     width = h1_block.shape[1]
 
     def attention(i):
         yield from ring_sum_steps(
-            ring, pieces[i], chunks[i], recvs[i], ring_send.at[i], ring_recv.at[i]
+            rings[(n_mlp + i) % 2], pieces[i], chunks[i], recvs[i], ring_send.at[i], ring_recv.at[i]
         )
         k = n_mlp + i
         yield from ring_gather_steps(
-            ring, plane, chunks[i], att_outs[i], row_sems.at[k], gather_send.at[k], gather_recv.at[k]
+            rings[(n_mlp + i) % 2], plane, chunks[i], att_outs[i], row_sems.at[k], gather_send.at[k], gather_recv.at[k]
         )
 
     def normed():
@@ -330,7 +332,7 @@
 
     gathers = [
         ring_gather_steps(
-            ring, plane, mlp_chunks[i], mlp_outs[i], row_sems.at[i], gather_send.at[i], gather_recv.at[i]
+            rings[i % 2], plane, mlp_chunks[i], mlp_outs[i], row_sems.at[i], gather_send.at[i], gather_recv.at[i]
         )
         for i in range(n_mlp)
     ]
@@ -528,8 +530,9 @@
     return grad.reshape(2, count, grad.shape[0] // (2 * count), grad.shape[1])
 
 
-def from_chunks(summed):
-    return summed.transpose(0, 2, 1, 3).reshape(-1, 2 * summed.shape[3]).astype(F32)
+def from_chunks(summed, turned):
+    halves = [summed[:, i].reshape(-1, summed.shape[3]).astype(F32) for i in range(2)]
+    return jnp.concatenate([half.T for half in halves]) if turned else jnp.concatenate(halves, 1)
 
 
 def on_device(
@@ -569,11 +572,12 @@
     gains = jnp.stack([norm1_gain, norm2_gain])
     gains = in_order(row, gains, swap_rows(gains), 1)
     w_o = whole_of_half(w_out, row, 0, 1)
+
+    token_full, cot_full = plane_gather([tokens, cotangent], 0)
+    token_full, w_gate, w_up, w_down = lax.optimization_barrier((token_full, w_gate, w_up, w_down))
     w_g = whole_of_half(w_gate, row, 1, 0)
     w_u = whole_of_half(w_up, row, 1, 0)
     w_d = whole_of_half(w_down, row, 0, 1)
-
-    token_full, cot_full = plane_gather([tokens, cotangent], 0)
     resid = token_full.astype(F32)
     unit_one, inverse_one = unit_of(resid)
     normed_one = (unit_one * gains[0:1]).astype(BF16)
@@ -646,7 +650,7 @@
     d_tokens = own_block(d_tokens.astype(BF16))
     own_small = lax.dynamic_index_in_dim(small, row, 0, keepdims=False)
     bias_sum = [small[:, 2 + i, :own_cols].reshape(-1) for i in range(3)]
-    summed = [from_chunks(item) for item in summed]
+    summed = [from_chunks(item, i in (2, 6)) for i, item in enumerate(summed)]
     return (
         layer_out,
         d_tokens,
@@ -657,11 +661,11 @@
         bias_sum[0],
         bias_sum[1],
         bias_sum[2],
-        summed[6].T,
+        summed[6],
         own_small[1],
         summed[0],
         summed[1],
-        summed[2].T,
+        summed[2],
     )
 
 

time: 290 us -> 283 us (0.976)
  Pallas kernels: 192 us -> 180 us
  waiting for transfers between devices: 0.02 us -> 10.2 us
  local copies, waits for them, and re-layouts: 38 us -> 27.9 us
  other arithmetic: 15.5 us -> 21.7 us
    pallas_call x1, Pallas kernels: 34.5 us -> 23 us  [plane_gather(): pl.pallas_call(functools.partial(gather_kernel, rows, cols, count), out_s...]
    ppermute x6, waiting for transfers between devices: 0.02 us -> 10.2 us  [swap_rows(): return lax.ppermute(value, 'row', [(0, 1), (1, 0)])]
    unnamed x165, local copies, waits for them, and re-layouts: 13.3 us -> 3.35 us
    concatenate x0 -> x7, other arithmetic: none -> 9.16 us  [the longest x5 7.01 us: from_chunks(): jnp.concatenate(halves, 1)]
  transfers between devices with their start and end apart: 6 -> 6, of which waited for: 0 -> 1; matrix products, arithmetic and copies ran while one was open for 6% -> 6% of each run, Pallas kernels for 19% -> 15%
where the time goes in v1:
time: 283 us; the launch traced here: 282 us
  Pallas kernels  180 us (64%)
  matrix products  33.7 us (12%)
  local copies, waits for them, and re-layouts  27.9 us (10%)
  other arithmetic  21.7 us (8%)
  waiting for transfers between devices  10.2 us (4%)
  starting transfers between devices  7.09 us (3%)
    pallas_call x3, Pallas kernels, call(): pl.pallas_call(kernel, out_shape=outs, in_specs=[VMEM] * len(ins), out_sp...  157 us
    pallas_call x1, Pallas kernels, plane_gather(): pl.pallas_call(functools.partial(gather_kernel, rows, cols, count), out_s...  23 us
    dot_general x9, matrix products, dot_right_t(): lax.dot_general(left, right, (((1,), (1,)), ((), ())), preferred_element_...  13.3 us
    dot_general x11, matrix products, dot_left_t(): lax.dot_general(left, right, (((0,), (0,)), ((), ())), preferred_element_...  10.4 us
    ppermute x6, waiting for transfers between devices, swap_rows(): return lax.ppermute(value, 'row', [(0, 1), (1, 0)])  10.2 us
    dot_general x9, matrix products, dot_plain(): return jnp.dot(left, right, preferred_element_type=F32)  9.97 us
    dynamic_slice x9, local copies, waits for them, and re-layouts, half_of(): return lax.dynamic_slice_in_dim(value, index * size, size, axis)  8.12 us
    ppermute x6, starting transfers between devices, swap_rows(): return lax.ppermute(value, 'row', [(0, 1), (1, 0)])  7.09 us
  transfers between devices with their start and end apart: 6, of which 1 were waited for; matrix products, arithmetic and copies ran while one was open for 6% of the time, Pallas kernels for 15%

profile of v1, /device:TPU:0, one launch (start us, length us, event | category | flops | bytes accessed | tf_op | source)
XLA Modules:
  0.0 282.5 jit_solution(8214607193358059436)
XLA Ops:
  2.4 1.8 constant_dynamic-slice_fusion.14
  5.1 2.9 %collective-permute-start.1 = (bf16[512,384]{1,0:T(8,128)(2,1)}, bf16[512,384]{1,0:T(8,128)(2,1)}, u32[]{:S(2)}, u32[]{:S(2)}) collective-permute-start(bf16[512,384]{1,0:T(8,128)(2,1)} %pad_maximum_fusion), channel_id=1, source_target_pairs={{0,4},{4,0},{1,5},{5,1},{2,6},{6,2},{3,7},{7,3},{8,12},{12,8},{9,1... | collective-permute-start | bytes 1179656 | tf_op jit(solution)/shard_map/ppermute | solution.py:466
  8.1 23.0 %plane_gather_0.1 = (bf16[512,1024]{1,0:T(8,128)(2,1)S(1)}, bf16[512,1024]{1,0:T(8,128)(2,1)S(1)}) custom-call(bf16[128,512]{1,0:T(8,128)(2,1)S(1)} %copy-done.9, bf16[128,512]{1,0:T(8,128)(2,1)S(1)} %copy-done.14), custom_call_target="tpu_custom_call" | custom-call | tf_op jit(solution)/shard_map/plane_gather_0/pallas_call | solution.py:365
  44.0 10.2 %collective-permute-done.3 = bf16[352,512]{1,0:T(8,128)(2,1)} collective-permute-done((bf16[352,512]{1,0:T(8,128)(2,1)}, bf16[352,512]{1,0:T(8,128)(2,1)}, u32[]{:S(2)}, u32[]{:S(2)}) %collective-permute-start.3) | collective-permute-done | bytes 360480 | tf_op jit(solution)/shard_map/ppermute | solution.py:466
  54.2 1.9 fusion.13
  56.2 1.9 fusion.167
  62.8 19.5 %out_projection_reduce.1 = bf16[512,1024]{1,0:T(8,128)(2,1)S(1)} custom-call(bf16[512,1024]{1,0:T(8,128)(2,1)S(1)} %convolution_convert_fusion.part, bf16[128,512]{1,0:T(8,128)(2,1)S(1)} %copy-done.9), custom_call_target="tpu_custom_call" | custom-call | tf_op jit(solution)/shard_map/out_projection_reduce/pallas_call | solution.py:393
  82.6 1.8 fusion.45
  84.5 1.8 multiply_convert_fusion.3
  88.6 2.3 copy.40
  90.9 2.5 convolution_convert_fusion.4
  93.4 2.3 copy.41
  95.6 2.7 convolution_convert_fusion.3
  98.4 2.3 copy.42
  100.7 2.2 fusion.46
  103.0 2.0 add_convert_fusion.refs_0_
  105.0 53.1 %mlp_back_reduce.1 = (bf16[512,1024]{1,0:T(8,128)(2,1)S(1)}, bf16[2,128,352]{2,1,0:T(8,128)(2,1)S(1)}, bf16[2,128,352]{2,1,0:T(8,128)(2,1)S(1)}, bf16[2,128,352]{2,1,0:T(8,128)(2,1)S(1)}) custom-call(bf16[512,1024]{1,0:T(8,128)(2,1)S(1)} %add_convert_fusion.refs_0_, bf16[2,4,128,352]{3,2,1,0:T(8,128)(2,1)S(1)} %bitcast.57, ...), custom_call_target="tpu_custom_call" | custom-call | tf_op jit(solution)/shard_map/mlp_back_reduce/pallas_call | solution.py:393
  159.9 1.9 convolution_convert_fusion.11
  173.4 1.9 convolution_convert_fusion.2.refs_0_
  175.3 1.9 convolution_convert_fusion.1.refs_1_
  177.3 84.4 %last_exchange.1 = (bf16[512,1024]{1,0:T(8,128)(2,1)S(1)}, bf16[128,512]{1,0:T(8,128)(2,1)S(1)}, f32[2,8,512]{2,1,0:T(8,128)S(1)}, bf16[4,2,128,352]{3,2,1,0:T(8...) custom-call(bf16[512,1024]{1,0:T(8,128)(2,1)S(1)} %convolution_conve, ...), custom_call_target="tpu_custom_call" | custom-call | tf_op jit(solution)/shard_map/last_exchange/pallas_call | solution.py:393
  261.7 1.9 multiply_reduce_fusion
  270.7 1.8 maximum_convert_fusion.3
  279.9 1.9 fusion.22
  (265 shorter events, 50.5 us)
Async XLA Ops:
  0.6 7.4 %copy-start.63 = (f32[512]{0:T(512)S(1)}, f32[512]{0:T(512)}, u32[]{:S(2)}) copy-start(f32[512]{0:T(512)} %param.29) | copy-start | bytes 6148
  0.7 7.4 %copy-start.64 = (f32[512]{0:T(512)S(1)}, f32[512]{0:T(512)}, u32[]{:S(2)}) copy-start(f32[512]{0:T(512)} %param.21) | copy-start | bytes 6148
  0.7 7.4 %copy-start.9 = (bf16[128,512]{1,0:T(8,128)(2,1)S(1)}, bf16[128,512]{1,0:T(8,128)(2,1)}, u32[]{:S(2)}) copy-start(bf16[128,512]{1,0:T(8,128)(2,1)} %addend.1) | copy-start | bytes 393220
  0.7 7.4 %copy-start.14 = (bf16[128,512]{1,0:T(8,128)(2,1)S(1)}, bf16[128,512]{1,0:T(8,128)(2,1)}, u32[]{:S(2)}) copy-start(bf16[128,512]{1,0:T(8,128)(2,1)} %refs_1_.1) | copy-start | bytes 393220
  0.7 30.5 %copy-start.23 = (bf16[512,704]{0,1:T(8,128)(2,1)S(1)}, bf16[512,704]{0,1:T(8,128)(2,1)}, u32[]{:S(2)}) copy-start(bf16[512,704]{0,1:T(8,128)(2,1)} %param.30) | copy-start | bytes 2162692
  4.3 33.9 %copy-start.75 = (f32[256]{0:T(256)S(1)}, f32[256]{0:T(256)}, u32[]{:S(2)}) copy-start(f32[256]{0:T(256)} %param.27) | copy-start | bytes 3076
  4.3 34.0 %copy-start.76 = (f32[256]{0:T(256)S(1)}, f32[256]{0:T(256)}, u32[]{:S(2)}) copy-start(f32[256]{0:T(256)} %param.26) | copy-start | bytes 3076
  4.3 34.1 %copy-start.77 = (f32[256]{0:T(256)S(1)}, f32[256]{0:T(256)}, u32[]{:S(2)}) copy-start(f32[256]{0:T(256)} %param.25) | copy-start | bytes 3076
  5.1 51.1 %collective-permute-start.1 = (bf16[512,384]{1,0:T(8,128)(2,1)}, bf16[512,384]{1,0:T(8,128)(2,1)}, u32[]{:S(2)}, u32[]{:S(2)}) collective-permute-start(bf16[512,384]{1,0:T(8,128)(2,1)} %pad_maximum_fusion), channel_id=1, source_target_pairs={{0,4},{4,0},{1,5},{5,1},{2,6},{6,2},{3,7},{7,3},{8,12},{12,8},{9,1... | collective-permute-start | bytes 1179656 | tf_op jit(solution)/shard_map/ppermute | solution.py:466
  8.0 35.4 %collective-permute-start = (f32[2,512]{1,0:T(2,128)S(1)}, f32[2,512]{1,0:T(2,128)S(1)}, u32[]{:S(2)}, u32[]{:S(2)}) collective-permute-start(f32[2,512]{1,0:T(2,128)S(1)} %pad_maximum_fusion.16), channel_id=1, source_target_pairs={{0,4},{4,0},{1,5},{5,1},{2,6},{6,2},{3,7},{7,3},{8,12},{12,8},{9,1... | collective-permute-start | bytes 12296 | tf_op jit(solution)/shard_map/ppermute | solution.py:466
  31.1 23.1 %copy-start = (bf16[512,1024]{1,0:T(8,128)(2,1)}, bf16[512,1024]{1,0:T(8,128)(2,1)S(1)}, u32[]{:S(2)}) copy-start(bf16[512,1024]{1,0:T(8,128)(2,1)S(1)} %get-tuple-element.60) | copy-start | bytes 3145732
  31.2 7.5 %copy-start.78 = (s32[1,3]{1,0:T(1,128)S(1)}, s32[1,3]{1,0:T(1,128)}, u32[]{:S(2)}) copy-start(s32[1,3]{1,0:T(1,128)} %param.20) | copy-start | bytes 40
  32.1 7.0 %copy-start.25 = (bf16[512,704]{0,1:T(8,128)(2,1)S(1)}, bf16[512,704]{0,1:T(8,128)(2,1)}, u32[]{:S(2)}) copy-start(bf16[512,704]{0,1:T(8,128)(2,1)} %param.31) | copy-start | bytes 2162692
  32.1 50.5 %collective-permute-start.5 = (bf16[512,352]{0,1:T(8,128)(2,1)}, bf16[512,352]{0,1:T(8,128)(2,1)}, u32[]{:S(2)}, u32[]{:S(2)}) collective-permute-start(bf16[512,352]{0,1:T(8,128)(2,1)} %get-tuple-element.118), channel_id=1, source_target_pairs={{0,4},{4,0},{1,5},{5,1},{2,6},{6,2},{3,7},{7,3},{8,12},{12,8},{9,1... | collective-permute-start | bytes 1081352 | tf_op jit(solution)/shard_map/ppermute | solution.py:466
  35.2 25.8 %copy-start.30 = (bf16[128,512]{1,0:T(8,128)(2,1)}, bf16[128,512]{1,0:T(8,128)(2,1)S(1)}, u32[]{:S(2)}) copy-start(bf16[128,512]{1,0:T(8,128)(2,1)S(1)} %get-tuple-element.129) | copy-start | bytes 393220
  35.2 25.8 %collective-permute-start.2 = (bf16[128,512]{1,0:T(8,128)(2,1)}, bf16[128,512]{1,0:T(8,128)(2,1)}, u32[]{:S(2)}, u32[]{:S(2)}) collective-permute-start(bf16[128,512]{1,0:T(8,128)(2,1)} %get-tuple-element.130), channel_id=1, source_target_pairs={{0,4},{4,0},{1,5},{5,1},{2,6},{6,2},{3,7},{7,3},{8,12},{12,8},{9,1... | collective-permute-start | bytes 393224 | tf_op jit(solution)/shard_map/ppermute | solution.py:466
  36.7 17.5 %collective-permute-start.3 = (bf16[352,512]{1,0:T(8,128)(2,1)}, bf16[352,512]{1,0:T(8,128)(2,1)}, u32[]{:S(2)}, u32[]{:S(2)}) collective-permute-start(bf16[352,512]{1,0:T(8,128)(2,1)} %get-tuple-element.120), channel_id=1, source_target_pairs={{0,4},{4,0},{1,5},{5,1},{2,6},{6,2},{3,7},{7,3},{8,12},{12,8},{9,1... | collective-permute-start | bytes 1081352 | tf_op jit(solution)/shard_map/ppermute | solution.py:466
  38.7 17.5 %copy-start.59 = (f32[512]{0:T(512)}, f32[512]{0:T(512)S(1)}, u32[]{:S(2)}) copy-start(f32[512]{0:T(512)S(1)} %add_rsqrt_fusion.1) | copy-start | bytes 6148
  43.5 41.0 %collective-permute-start.4 = (bf16[512,352]{0,1:T(8,128)(2,1)}, bf16[512,352]{0,1:T(8,128)(2,1)S(1)}, u32[]{:S(2)}, u32[]{:S(2)}) collective-permute-start(bf16[512,352]{0,1:T(8,128)(2,1)} %get-tuple-element.116), channel_id=1, source_target_pairs={{0,4},{4,0},{1,5},{5,1},{2,6},{6,2},{3,7},{7,3},{8,12},{12,8},{9,1... | collective-permute-start | bytes 1081352 | tf_op jit(solution)/shard_map/ppermute | solution.py:466
  44.0 12.2 %copy-start.61 = (f32[1,1024]{1,0:T(1,128)}, f32[1,1024]{1,0:T(1,128)S(1)}, u32[]{:S(2)}) copy-start(f32[1,1024]{1,0:T(1,128)S(1)} %get-tuple-element.143) | copy-start | bytes 12292
  61.0 21.6 %copy-start.57 = (bf16[512,64]{0,1:T(8,128)(2,1)}, bf16[512,64]{0,1:T(8,128)(2,1)S(1)}, u32[]{:S(2)}) copy-start(bf16[512,64]{0,1:T(8,128)(2,1)S(1)} %convolution_convert_fusion.13) | copy-start | bytes 196612
  61.3 21.3 %copy-start.33 = (bf16[512,352]{0,1:T(8,128)(2,1)S(1)}, bf16[512,352]{0,1:T(8,128)(2,1)}, u32[]{:S(2)}) copy-start(bf16[512,352]{0,1:T(8,128)(2,1)} %get-tuple-element.117) | copy-start | bytes 1081348
  105.0 54.0 %copy-start.1 = (bf16[512,1024]{1,0:T(8,128)(2,1)S(1)}, bf16[512,1024]{1,0:T(8,128)(2,1)}, u32[]{:S(2)}) copy-start(bf16[512,1024]{1,0:T(8,128)(2,1)} %copy-done) | copy-start | bytes 3145732
  159.9 6.8 %copy-start.17 = (f32[512,1024]{1,0:T(8,128)}, f32[512,1024]{1,0:T(8,128)S(1)}, u32[]{:S(2)}) copy-start(f32[512,1024]{1,0:T(8,128)S(1)} %fusion.5) | copy-start | bytes 6291460
  (64 other events, 123.6 us)

commit v2 on v1

--- a/solution.py
+++ b/solution.py
@@ -598,13 +598,14 @@
         head_outs.append(dot_plain(probs.astype(BF16), values).astype(BF16))
     heads = jnp.concatenate(head_outs, 1)
     h1_full = plane_reduce(dot_plain(heads, w_o).astype(BF16), tokens)
+    h1_full, late_cot = lax.optimization_barrier((h1_full, cot_full))
     unit_two, inverse_two = unit_of(h1_full.astype(F32))
     normed_two = (unit_two * gains[1:2]).astype(BF16)
     gate, upper = dot_plain(normed_two, w_g), dot_plain(normed_two, w_u)
     sigmoid_gate = jax.nn.sigmoid(gate)
     silu_gate = gate * sigmoid_gate
     hidden = (silu_gate * upper).astype(BF16)
-    d_hidden = dot_right_t(cot_full, w_d).astype(BF16).astype(F32)
+    d_hidden = dot_right_t(late_cot, w_d).astype(BF16).astype(F32)
     d_gate = (d_hidden * upper * sigmoid_gate * (1.0 + gate * (1.0 - sigmoid_gate))).astype(BF16)
     d_upper = (d_hidden * silu_gate).astype(BF16)
     part = (dot_right_t(d_gate, w_g) + dot_right_t(d_upper, w_u)).astype(BF16)

time: 283 us -> 279 us (0.986)
  waiting for transfers between devices: 10.2 us -> 0.02 us
  Pallas kernels: 180 us -> 185 us
    ppermute x6, waiting for transfers between devices: 10.2 us -> 0.02 us  [swap_rows(): return lax.ppermute(value, 'row', [(0, 1), (1, 0)])]
    pallas_call x3, Pallas kernels: 157 us -> 162 us  [call(): pl.pallas_call(kernel, out_shape=outs, in_specs=[VMEM] * len(ins), out_sp...]
  transfers between devices with their start and end apart: 6 -> 6, of which waited for: 1 -> 0; matrix products, arithmetic and copies ran while one was open for 6% -> 6% of each run, Pallas kernels for 15% -> 17%
where the time goes in v2:
time: 279 us; the launch traced here: 278 us
  Pallas kernels  185 us (66%)
  matrix products  33.4 us (12%)
  local copies, waits for them, and re-layouts  29.6 us (11%)
  other arithmetic  20.9 us (7%)
  starting transfers between devices  7.18 us (3%)
    pallas_call x3, Pallas kernels, call(): pl.pallas_call(kernel, out_shape=outs, in_specs=[VMEM] * len(ins), out_sp...  162 us
    pallas_call x1, Pallas kernels, plane_gather(): pl.pallas_call(functools.partial(gather_kernel, rows, cols, count), out_s...  22.8 us
    dot_general x9, matrix products, dot_right_t(): lax.dot_general(left, right, (((1,), (1,)), ((), ())), preferred_element_...  13.1 us
    dot_general x11, matrix products, dot_left_t(): lax.dot_general(left, right, (((0,), (0,)), ((), ())), preferred_element_...  10.4 us
    dot_general x9, matrix products, dot_plain(): return jnp.dot(left, right, preferred_element_type=F32)  9.88 us
    dynamic_slice x9, local copies, waits for them, and re-layouts, half_of(): return lax.dynamic_slice_in_dim(value, index * size, size, axis)  8.23 us
    ppermute x6, starting transfers between devices, swap_rows(): return lax.ppermute(value, 'row', [(0, 1), (1, 0)])  7.18 us
    concatenate x5, other arithmetic, from_chunks(): jnp.concatenate(halves, 1)  7.01 us
  transfers between devices with their start and end apart: 6, of which 0 were waited for; matrix products, arithmetic and copies ran while one was open for 6% of the time, Pallas kernels for 17%

profile of v2, /device:TPU:0, one launch (start us, length us, event | category | flops | bytes accessed | tf_op | source)
XLA Modules:
  0.0 278.2 jit_solution(570846928930707620)
XLA Ops:
  0.7 1.7 constant_dynamic-slice_fusion.16
  2.4 1.9 constant_dynamic-slice_fusion.14
  4.4 3.0 %collective-permute-start.1 = (bf16[512,384]{1,0:T(8,128)(2,1)S(1)}, bf16[512,384]{1,0:T(8,128)(2,1)}, u32[]{:S(2)}, u32[]{:S(2)}) collective-permute-start(bf16[512,384]{1,0:T(8,128)(2,1)S(1)} %pad_maximum_fusion), channel_id=1, source_target_pairs={{0,4},{4,0},{1,5},{5,1},{2,6},{6,2},{3,7},{7,3},{8,12},{12,8},{9,1... | collective-permute-start | bytes 1179656 | tf_op jit(solution)/shard_map/ppermute | solution.py:466
  7.5 22.8 %plane_gather_0.1 = (bf16[512,1024]{1,0:T(8,128)(2,1)S(1)}, bf16[512,1024]{1,0:T(8,128)(2,1)S(1)}) custom-call(bf16[128,512]{1,0:T(8,128)(2,1)S(1)} %copy-done.10, bf16[128,512]{1,0:T(8,128)(2,1)S(1)} %copy-done.15), custom_call_target="tpu_custom_call" | custom-call | tf_op jit(solution)/shard_map/plane_gather_0/pallas_call | solution.py:365
  44.2 1.9 fusion.167
  51.4 24.4 %out_projection_reduce.1 = bf16[512,1024]{1,0:T(8,128)(2,1)S(1)} custom-call(bf16[512,1024]{1,0:T(8,128)(2,1)S(1)} %convolution_convert_fusion.part, bf16[128,512]{1,0:T(8,128)(2,1)S(1)} %copy-done.10), custom_call_target="tpu_custom_call" | custom-call | tf_op jit(solution)/shard_map/out_projection_reduce/pallas_call | solution.py:393
  77.8 1.8 fusion.45
  79.7 1.8 multiply_convert_fusion.3
  83.8 2.3 copy.40
  86.1 2.5 convolution_convert_fusion.4
  88.6 2.3 copy.41
  90.9 2.7 convolution_convert_fusion.3
  93.6 2.3 copy.42
  95.9 2.2 fusion.46
  98.2 2.0 add_convert_fusion.refs_0_
  100.3 53.2 %mlp_back_reduce.1 = (bf16[512,1024]{1,0:T(8,128)(2,1)S(1)}, bf16[2,128,352]{2,1,0:T(8,128)(2,1)S(1)}, bf16[2,128,352]{2,1,0:T(8,128)(2,1)S(1)}, bf16[2,128,352]{2,1,0:T(8,128)(2,1)S(1)}) custom-call(bf16[512,1024]{1,0:T(8,128)(2,1)S(1)} %add_convert_fusion.refs_0_, bf16[2,4,128,352]{3,2,1,0:T(8,128)(2,1)S(1)} %bitcast.57, ...), custom_call_target="tpu_custom_call" | custom-call | tf_op jit(solution)/shard_map/mlp_back_reduce/pallas_call | solution.py:393
  155.2 1.9 convolution_convert_fusion.11
  168.7 1.9 convolution_convert_fusion.2.refs_0_
  170.7 1.9 convolution_convert_fusion.1.refs_1_
  172.6 84.8 %last_exchange.1 = (bf16[512,1024]{1,0:T(8,128)(2,1)S(1)}, bf16[128,512]{1,0:T(8,128)(2,1)S(1)}, f32[2,8,512]{2,1,0:T(8,128)S(1)}, bf16[4,2,128,352]{3,2,1,0:T(8...) custom-call(bf16[512,1024]{1,0:T(8,128)(2,1)S(1)} %convolution_conve, ...), custom_call_target="tpu_custom_call" | custom-call | tf_op jit(solution)/shard_map/last_exchange/pallas_call | solution.py:393
  257.4 1.9 multiply_reduce_fusion
  266.5 1.8 maximum_convert_fusion.3
  268.3 1.8 maximum_convert_fusion.4
  275.7 1.9 fusion.22
  (269 shorter events, 49.6 us)
Async XLA Ops:
  0.6 6.8 %copy-start.65 = (f32[512]{0:T(512)S(1)}, f32[512]{0:T(512)}, u32[]{:S(2)}) copy-start(f32[512]{0:T(512)} %param.29) | copy-start | bytes 6148
  0.7 6.8 %copy-start.66 = (f32[512]{0:T(512)S(1)}, f32[512]{0:T(512)}, u32[]{:S(2)}) copy-start(f32[512]{0:T(512)} %param.21) | copy-start | bytes 6148
  0.7 6.9 %copy-start.10 = (bf16[128,512]{1,0:T(8,128)(2,1)S(1)}, bf16[128,512]{1,0:T(8,128)(2,1)}, u32[]{:S(2)}) copy-start(bf16[128,512]{1,0:T(8,128)(2,1)} %addend.1) | copy-start | bytes 393220
  0.7 6.8 %copy-start.15 = (bf16[128,512]{1,0:T(8,128)(2,1)S(1)}, bf16[128,512]{1,0:T(8,128)(2,1)}, u32[]{:S(2)}) copy-start(bf16[128,512]{1,0:T(8,128)(2,1)} %refs_1_.1) | copy-start | bytes 393220
  0.7 30.6 %copy-start.24 = (bf16[512,704]{0,1:T(8,128)(2,1)S(1)}, bf16[512,704]{0,1:T(8,128)(2,1)}, u32[]{:S(2)}) copy-start(bf16[512,704]{0,1:T(8,128)(2,1)} %param.30) | copy-start | bytes 2162692
  2.4 33.5 %copy-start.25 = (bf16[704,512]{1,0:T(8,128)(2,1)S(1)}, bf16[704,512]{1,0:T(8,128)(2,1)}, u32[]{:S(2)}) copy-start(bf16[704,512]{1,0:T(8,128)(2,1)} %param.32) | copy-start | bytes 2162692
  4.3 34.0 %copy-start.77 = (f32[256]{0:T(256)S(1)}, f32[256]{0:T(256)}, u32[]{:S(2)}) copy-start(f32[256]{0:T(256)} %param.27) | copy-start | bytes 3076
  4.3 34.0 %copy-start.78 = (f32[256]{0:T(256)S(1)}, f32[256]{0:T(256)}, u32[]{:S(2)}) copy-start(f32[256]{0:T(256)} %param.26) | copy-start | bytes 3076
  4.3 34.1 %copy-start.79 = (f32[256]{0:T(256)S(1)}, f32[256]{0:T(256)}, u32[]{:S(2)}) copy-start(f32[256]{0:T(256)} %param.25) | copy-start | bytes 3076
  4.4 39.8 %collective-permute-start.1 = (bf16[512,384]{1,0:T(8,128)(2,1)S(1)}, bf16[512,384]{1,0:T(8,128)(2,1)}, u32[]{:S(2)}, u32[]{:S(2)}) collective-permute-start(bf16[512,384]{1,0:T(8,128)(2,1)S(1)} %pad_maximum_fusion), channel_id=1, source_target_pairs={{0,4},{4,0},{1,5},{5,1},{2,6},{6,2},{3,7},{7,3},{8,12},{12,8},{9,1... | collective-permute-start | bytes 1179656 | tf_op jit(solution)/shard_map/ppermute | solution.py:466
  7.4 36.1 %collective-permute-start = (f32[2,512]{1,0:T(2,128)S(1)}, f32[2,512]{1,0:T(2,128)S(1)}, u32[]{:S(2)}, u32[]{:S(2)}) collective-permute-start(f32[2,512]{1,0:T(2,128)S(1)} %pad_maximum_fusion.16), channel_id=1, source_target_pairs={{0,4},{4,0},{1,5},{5,1},{2,6},{6,2},{3,7},{7,3},{8,12},{12,8},{9,1... | collective-permute-start | bytes 12296 | tf_op jit(solution)/shard_map/ppermute | solution.py:466
  31.3 7.5 %copy-start.80 = (s32[1,3]{1,0:T(1,128)S(1)}, s32[1,3]{1,0:T(1,128)}, u32[]{:S(2)}) copy-start(s32[1,3]{1,0:T(1,128)} %param.20) | copy-start | bytes 40
  32.2 7.0 %copy-start.26 = (bf16[512,704]{0,1:T(8,128)(2,1)S(1)}, bf16[512,704]{0,1:T(8,128)(2,1)}, u32[]{:S(2)}) copy-start(bf16[512,704]{0,1:T(8,128)(2,1)} %param.31) | copy-start | bytes 2162692
  32.2 45.6 %collective-permute-start.5 = (bf16[512,352]{0,1:T(8,128)(2,1)}, bf16[512,352]{0,1:T(8,128)(2,1)}, u32[]{:S(2)}, u32[]{:S(2)}) collective-permute-start(bf16[512,352]{0,1:T(8,128)(2,1)} %get-tuple-element.122), channel_id=1, source_target_pairs={{0,4},{4,0},{1,5},{5,1},{2,6},{6,2},{3,7},{7,3},{8,12},{12,8},{9,1... | collective-permute-start | bytes 1081352 | tf_op jit(solution)/shard_map/ppermute | solution.py:466
  35.4 14.0 %copy-start.31 = (bf16[128,512]{1,0:T(8,128)(2,1)}, bf16[128,512]{1,0:T(8,128)(2,1)S(1)}, u32[]{:S(2)}) copy-start(bf16[128,512]{1,0:T(8,128)(2,1)S(1)} %get-tuple-element.133) | copy-start | bytes 393220
  35.4 14.0 %collective-permute-start.2 = (bf16[128,512]{1,0:T(8,128)(2,1)}, bf16[128,512]{1,0:T(8,128)(2,1)}, u32[]{:S(2)}, u32[]{:S(2)}) collective-permute-start(bf16[128,512]{1,0:T(8,128)(2,1)} %get-tuple-element.134), channel_id=1, source_target_pairs={{0,4},{4,0},{1,5},{5,1},{2,6},{6,2},{3,7},{7,3},{8,12},{12,8},{9,1... | collective-permute-start | bytes 393224 | tf_op jit(solution)/shard_map/ppermute | solution.py:466
  36.8 38.9 %collective-permute-start.3 = (bf16[352,512]{1,0:T(8,128)(2,1)}, bf16[352,512]{1,0:T(8,128)(2,1)}, u32[]{:S(2)}, u32[]{:S(2)}) collective-permute-start(bf16[352,512]{1,0:T(8,128)(2,1)} %get-tuple-element.124), channel_id=1, source_target_pairs={{0,4},{4,0},{1,5},{5,1},{2,6},{6,2},{3,7},{7,3},{8,12},{12,8},{9,1... | collective-permute-start | bytes 1081352 | tf_op jit(solution)/shard_map/ppermute | solution.py:466
  43.6 36.1 %collective-permute-start.4 = (bf16[512,352]{0,1:T(8,128)(2,1)}, bf16[512,352]{0,1:T(8,128)(2,1)S(1)}, u32[]{:S(2)}, u32[]{:S(2)}) collective-permute-start(bf16[512,352]{0,1:T(8,128)(2,1)} %get-tuple-element.120), channel_id=1, source_target_pairs={{0,4},{4,0},{1,5},{5,1},{2,6},{6,2},{3,7},{7,3},{8,12},{12,8},{9,1... | collective-permute-start | bytes 1081352 | tf_op jit(solution)/shard_map/ppermute | solution.py:466
  49.3 26.5 %copy-start.1 = (bf16[512,1024]{1,0:T(8,128)(2,1)S(1)}, bf16[512,1024]{1,0:T(8,128)(2,1)}, u32[]{:S(2)}) copy-start(bf16[512,1024]{1,0:T(8,128)(2,1)} %copy-done) | copy-start | bytes 3145732
  49.3 26.4 %copy-start.33 = (bf16[352,512]{1,0:T(8,128)(2,1)S(1)}, bf16[352,512]{1,0:T(8,128)(2,1)}, u32[]{:S(2)}) copy-start(bf16[352,512]{1,0:T(8,128)(2,1)} %get-tuple-element.123) | copy-start | bytes 1081348
  100.2 54.0 %copy-start.2 = (bf16[512,1024]{1,0:T(8,128)(2,1)S(1)}, bf16[512,1024]{1,0:T(8,128)(2,1)}, u32[]{:S(2)}) copy-start(bf16[512,1024]{1,0:T(8,128)(2,1)} %copy-done) | copy-start | bytes 3145732
  155.2 6.8 %copy-start.18 = (f32[512,1024]{1,0:T(8,128)}, f32[512,1024]{1,0:T(8,128)S(1)}, u32[]{:S(2)}) copy-start(f32[512,1024]{1,0:T(8,128)S(1)} %fusion.5) | copy-start | bytes 6291460
  265.5 5.4 %copy-start.27 = (bf16[512,128]{0,1:T(8,128)(2,1)S(1)}, bf16[512,128]{0,1:T(8,128)(2,1)}, u32[]{:S(2)}) copy-start(bf16[512,128]{0,1:T(8,128)(2,1)} %copy.44) | copy-start | bytes 393220
  265.7 6.1 %copy-start.23 = (bf16[512,352]{0,1:T(8,128)(2,1)S(1)}, bf16[512,352]{0,1:T(8,128)(2,1)}, u32[]{:S(2)}) copy-start(bf16[512,352]{0,1:T(8,128)(2,1)} %copy.46) | copy-start | bytes 1081348
  (66 other events, 127.8 us)
